TPU v7x, 32 devices: a whole 2x2x4 slice. The times are simulated.
32 devices in a mesh: shot: 2 (over y), gx: 4 (over z), section: 2 (over x), gy: 2 (over core).
Axes of the slice: x: 2, y: 2, z: 4, core: 2. Of those that a mesh axis runs over, the one named last changes fastest.
Arguments:
- wave_now: float32 [256, 32, 512], P(('shot', 'gx'), 'section', 'gy'), parts along dimension 0, may hold values from -6 to 6
- wave_before: float32 [256, 32, 512], P(('shot', 'gx'), 'section', 'gy'), parts along dimension 0, may hold values from -6 to 6
- courant: float32 [256, 32, 512], P(('shot', 'gx'), 'section', 'gy'), parts along dimension 0, may hold values from 0.03 to 0.12
- anisotropy: float32 [256, 32, 512], P(('shot', 'gx'), 'section', 'gy'), parts along dimension 0, may hold values from 0 to 0.3
- tilt: float32 [256, 32, 512], P(('shot', 'gx'), 'section', 'gy'), parts along dimension 0, may hold values from -3.140625 to 3.140625
- reflectivity: bfloat16 [17, 256, 32, 512], P(None, ('shot', 'gx'), 'section', 'gy'), parts along dimension 1, may hold values from -2.5 to 2.5
- offsets: int32 [17], replicated, may hold values from -16 to 16, as said below
Outputs:
- background: float32 [256, 32, 512], P(('shot', 'gx'), 'section', 'gy'), parts along dimension 0
- scattered: float32 [256, 32, 512], P(('shot', 'gx'), 'section', 'gy'), parts along dimension 0
There are 2 independent parts, one for each index of `shot`. A program takes and returns all parts, laid end to end along the dimension named above; an argument that names none is the same for every part. Nothing has to cross between parts.
Inputs may be any that keep to these rules, and one draw needn't show every extreme that they name: 17 distinct offsets, among them 0, -16 and 16.
All inputs are finite; a program needn't handle non-finite values.
Results may differ from a plain program's by a relative error of at most 0.0003.
Values sent between devices are 32-bit elements; how exact they have to be, the bound alone decides.
A program may use at most 64 MiB of HBM per device.

v0:
```python
import jax
import jax.numpy as jnp
from jax import lax
from jax.sharding import PartitionSpec as P

NOFF = 17
MARGIN = 16
ROUNDS = 3
STEPS = 2


def padded_2(cells, sides, width):
    for axis, dim in sides:
        count = lax.axis_size(axis)
        ends = count - 1
        head = lax.slice_in_dim(cells, 0, width, axis=dim)
        tail = lax.slice_in_dim(cells, cells.shape[dim] - width, cells.shape[dim], axis=dim)
        cells = jnp.concatenate(
            [
                lax.ppermute(tail, axis, [(i, (i + 1) % count) for i in range(ends)]),
                cells,
                lax.ppermute(head, axis, [((i + 1) % count, i) for i in range(ends)]),
            ],
            axis=dim,
        )
    return cells


def coefficients(courant, anisotropy, tilt):
    sine_tilt = jnp.sin(tilt)
    cosine_tilt = jnp.cos(tilt)
    stretch = 1.0 + 2.0 * anisotropy
    coef_xx = courant * (stretch * cosine_tilt * cosine_tilt + sine_tilt * sine_tilt)
    coef_zz = courant * (stretch * sine_tilt * sine_tilt + cosine_tilt * cosine_tilt)
    coef_yy = courant * stretch
    coef_xz = courant * 4.0 * anisotropy * sine_tilt * cosine_tilt
    return (coef_xx, coef_zz, coef_yy, coef_xz)


def apply_operator(padded, coef_set):
    centre = padded[1:-1, 1:-1, 1:-1]
    diff_xx = padded[2:, 1:-1, 1:-1] + padded[:-2, 1:-1, 1:-1] - 2.0 * centre
    diff_zz = padded[1:-1, 2:, 1:-1] + padded[1:-1, :-2, 1:-1] - 2.0 * centre
    diff_yy = padded[1:-1, 1:-1, 2:] + padded[1:-1, 1:-1, :-2] - 2.0 * centre
    diff_xz = 0.25 * (
        padded[2:, 2:, 1:-1]
        - padded[2:, :-2, 1:-1]
        - padded[:-2, 2:, 1:-1]
        + padded[:-2, :-2, 1:-1]
    )
    return (
        coef_set[0] * diff_xx
        + coef_set[1] * diff_zz
        + coef_set[2] * diff_yy
        + coef_set[3] * diff_xz
    )


def step_single(current, prior, coef_set):
    padded = padded_2(current, (("gx", 0), ("section", 1), ("gy", 2)), 1)
    return 2.0 * current - prior + apply_operator(padded, coef_set)


def shards(wave_now, wave_before, courant, anisotropy, tilt, reflectivity, offsets):
    cells_x = wave_now.shape[0]
    core_coefs = coefficients(courant, anisotropy, tilt)
    current = wave_now
    prior = wave_before
    wave_scat = jnp.zeros_like(wave_now)
    scat_prior = jnp.zeros_like(wave_now)
    for round_index in range(ROUNDS):
        run_current = current
        run_prior = prior
        for run_step_index in range(STEPS):
            run_advanced = step_single(run_current, run_prior, core_coefs)
            run_prior = run_current
            run_current = run_advanced
        current = run_current
        prior = run_prior
        extended = padded_2(current, (("gx", 0),), MARGIN)

        def accumulate(offset_index, running):
            start = MARGIN + offsets[offset_index]
            moved = lax.dynamic_slice_in_dim(extended, start, cells_x, 0)
            return running + reflectivity[offset_index].astype(jnp.float32) * moved

        source = lax.fori_loop(0, NOFF, accumulate, jnp.zeros_like(current))
        source, forcing = (source, courant * source)
        run_wave_scat = wave_scat
        run_scat_prior = scat_prior
        for step_index in range(STEPS):
            advanced = step_single(run_wave_scat, run_scat_prior, core_coefs) + forcing
            run_scat_prior = run_wave_scat
            run_wave_scat = advanced
        wave_scat = run_wave_scat
        scat_prior = run_scat_prior
    return (current, wave_scat)


def solution(mesh):
    return jax.shard_map(
        shards,
        mesh=mesh,
        in_specs=(
            P(("shot", "gx"), "section", "gy"),
            P(("shot", "gx"), "section", "gy"),
            P(("shot", "gx"), "section", "gy"),
            P(("shot", "gx"), "section", "gy"),
            P(("shot", "gx"), "section", "gy"),
            P(None, ("shot", "gx"), "section", "gy"),
            P(),
        ),
        out_specs=(P(("shot", "gx"), "section", "gy"), P(("shot", "gx"), "section", "gy")),
        check_vma=False,
    )
```

profile of v0, /device:TPU:0, one launch (start us, length us, event | category | flops | bytes accessed | tf_op | source)
XLA Modules:
  0.0 483.3 jit_solution(8201738399693499562)
XLA Ops:
  1.6 4.9 %collective-permute-start.1 = (f32[1,16,256]{2,1,0:T(8,128)S(1)}, f32[1,16,256]{2,1,0:T(8,128)S(1)}, u32[]{:S(2)}, u32[]{:S(2)}) collective-permute-start(f32[1,16,256]{2,1,0:T(8,128)S(1)} %get-tuple-element.595), channel_id=1, source_target_pairs={{0,4},{4,8},{8,12},{1,5},{5,9},{9,13},{2,6},{6,10},{10,14},{3,7},{... | collective-permute-start | bytes 49160 | tf_op jit(solution)/shard_map/ppermute | solution.py:20
  9.0 3.1 collective-permute-done
  13.5 4.5 collective-permute-start.3
  21.2 3.1 collective-permute-start.5
  26.3 2.5 fusion.20
  30.1 4.5 collective-permute-start.7
  37.4 4.5 collective-permute-start.9
  43.3 4.8 collective-permute-start.37
  49.8 3.1 collective-permute-start.11
  56.3 4.6 collective-permute-start.13
  62.3 4.5 collective-permute-start.39
  68.3 4.5 collective-permute-start.15
  76.0 3.1 collective-permute-start.17
  82.6 4.6 collective-permute-start.19
  89.5 4.6 collective-permute-start.41
  95.5 4.5 collective-permute-start.21
  103.3 3.1 collective-permute-start.23
  109.8 4.6 collective-permute-start.25
  114.4 3.9 collective-permute-start.42
  119.7 4.5 collective-permute-start.27
  126.4 5.3 %collective-permute-start.56 = (f32[16,16,256]{2,1,0:T(8,128)}, f32[16,16,256]{2,1,0:T(8,128)}, u32[]{:S(2)}, u32[]{:S(2)}) collective-permute-start(f32[16,16,256]{2,1,0:T(8,128)} %get-tuple-element.574), channel_id=1, source_target_pairs={{0,4},{4,8},{8,12},{1,5},{5,9},{9,13},{2,6},{6,10},{10,14},{3,7},{... | collective-permute-start | bytes 786440 | tf_op jit(solution)/shard_map/ppermute | solution.py:20
  137.9 70.0 %while.48 = (s32[]{:T(128)}, f32[32,16,256]{2,1,0:T(8,128)}, bf16[17,32,16,256]{3,2,1,0:T(8,128)(2,1)}, s32[17]{0:T(128)S(1)}, f32[64,16,256]{2,1,0:T(8,128)}, /...) while((s32[]{:T(128)}, f32[32,16,256]{2,1,0:T(8,128)}, bf16[17,32,16,256]{3,2,1,0:T(8,128)(2,1)}, ...), condition=%wide.region_1.0_spmd.clone, body=%wide.region_0.0_spmd.clone.sunk | while | flops 524295 | bytes 1835177 | solution.py:87
  207.9 4.1 collective-permute-start.29
  212.0 4.1 fusion.8
  217.5 5.2 %collective-permute-start.45 = (f32[1,16,256]{2,1,0:T(8,128)S(1)}, f32[1,16,256]{2,1,0:T(8,128)S(1)}, u32[]{:S(2)}, u32[]{:S(2)}) collective-permute-start(f32[1,16,256]{2,1,0:T(8,128)S(1)} %get-tuple-element.578), channel_id=1, source_target_pairs={{0,4},{4,8},{8,12},{1,5},{5,9},{9,13},{2,6},{6,10},{10,14},{3,7},{... | collective-permute-start | bytes 49160 | tf_op jit(solution)/shard_map/ppermute | solution.py:20
  225.8 4.5 collective-permute-start.47
  233.6 3.1 collective-permute-start.49
  236.8 4.3 collective-permute-start.31
  243.3 4.6 collective-permute-start.51
  249.2 4.5 collective-permute-start.33
  255.1 4.7 collective-permute-start.53
  263.9 4.6 collective-permute-start.55
  272.0 55.4 %while.49 = (s32[]{:T(128)}, f32[32,16,256]{2,1,0:T(8,128)S(1)}, bf16[17,32,16,256]{3,2,1,0:T(8,128)(2,1)}, s32[17]{0:T(128)S(1)}, f32[64,16,256]{2,1,0:T(8,128)...) while((s32[]{:T(128)}, f32[32,16,256]{2,1,0:T(8,128)S(1)}, ...), condition=%wide.region_3.0_spmd.clone, body=%wide.region_2.0_spmd.clone.sunk | while | flops 524295 | bytes 1835177 | solution.py:87
  328.2 5.0 %fusion.75 = (f32[32,16,256]{2,1,0:T(8,128)S(1)}, f32[32,16,256]{2,1,0:T(8,128)S(1)}) fusion(f32[32,16,256]{2,1,0:T(8,128)S(1)} %get-tuple-element.495, f32[34,17,256]{2,1,0:T(8,128)} %get-tuple-element.533, f32[34,17,256]{2,1,0:T(8,128)} %get-tuple-element.532, f32[32,16,256]{2,1,0:T(8,128)S(1)} %get-tuple-element.493, ...), kind=kLoop, calls=%fused_computation.182 | loop fusion | flops 4456448 | bytes 8495904 | tf_op jit(solution)/shard_map/add | solution.py:92
  334.5 4.6 collective-permute-start.59
  340.7 3.1 collective-permute-start.35
  345.2 4.5 collective-permute-start.61
  352.9 3.1 collective-permute-start.63
  359.6 4.6 collective-permute-start.65
  366.9 4.5 collective-permute-start.67
  371.5 4.2 collective-permute-start.70
  379.6 4.6 collective-permute-start.69
  386.5 69.7 %while.50 = (s32[]{:T(128)}, f32[32,16,256]{2,1,0:T(8,128)}, bf16[17,32,16,256]{3,2,1,0:T(8,128)(2,1)}, s32[17]{0:T(128)S(1)}, f32[64,16,256]{2,1,0:T(8,128)}, /...) while((s32[]{:T(128)}, f32[32,16,256]{2,1,0:T(8,128)}, bf16[17,32,16,256]{3,2,1,0:T(8,128)(2,1)}, ...), condition=%wide.region_5.0_spmd.clone, body=%wide.region_4.0_spmd.clone.sunk | while | flops 524295 | bytes 1835177 | solution.py:87
  400.6 2.2 fusion.212
  456.3 4.0 fusion.47
  461.5 5.2 %collective-permute-start.73 = (f32[1,16,256]{2,1,0:T(8,128)S(1)}, f32[1,16,256]{2,1,0:T(8,128)S(1)}, u32[]{:S(2)}, u32[]{:S(2)}) collective-permute-start(f32[1,16,256]{2,1,0:T(8,128)S(1)} %get-tuple-element.566), channel_id=1, source_target_pairs={{0,4},{4,8},{8,12},{1,5},{5,9},{9,13},{2,6},{6,10},{10,14},{3,7},{... | collective-permute-start | bytes 49160 | tf_op jit(solution)/shard_map/ppermute | solution.py:20
  469.5 4.5 collective-permute-start.75
  477.2 3.1 collective-permute-start.77
  (338 shorter events, 227.9 us)
Async XLA Ops:
  36.1 12.0 %collective-permute-start.8 = (f32[34,1,256]{2,1,0:T(1,128)S(1)}, f32[34,1,256]{2,1,0:T(1,128)S(1)}, u32[]{:S(2)}, u32[]{:S(2)}) collective-permute-start(f32[34,1,256]{2,1,0:T(1,128)S(1)} %get-tuple-element.562), channel_id=1, source_target_pairs={{2,0},{3,1},{6,4},{7,5},{10,8},{11,9},{14,12},{15,13},{18,16},{19,... | collective-permute-start | bytes 104456 | tf_op jit(solution)/shard_map/ppermute | solution.py:22
  37.4 10.7 %collective-permute-start.9 = (f32[34,1,256]{2,1,0:T(1,128)S(1)}, f32[34,1,256]{2,1,0:T(1,128)S(1)}, u32[]{:S(2)}, u32[]{:S(2)}) collective-permute-start(f32[34,1,256]{2,1,0:T(1,128)S(1)} %get-tuple-element.563), channel_id=1, source_target_pairs={{0,2},{1,3},{4,6},{5,7},{8,10},{9,11},{12,14},{13,15},{16,18},{17,... | collective-permute-start | bytes 104456 | tf_op jit(solution)/shard_map/ppermute | solution.py:20
  42.0 18.9 %collective-permute-start.36 = (f32[1,16,256]{2,1,0:T(8,128)S(1)}, f32[1,16,256]{2,1,0:T(8,128)S(1)}, u32[]{:S(2)}, u32[]{:S(2)}) collective-permute-start(f32[1,16,256]{2,1,0:T(8,128)S(1)} %broadcast.18), channel_id=1, source_target_pairs={{4,0},{8,4},{12,8},{5,1},{9,5},{13,9},{6,2},{10,6},{14,10},{7,3},{... | collective-permute-start | bytes 49160 | tf_op jit(solution)/shard_map/ppermute | solution.py:22
  43.3 17.6 %collective-permute-start.37 = (f32[1,16,256]{2,1,0:T(8,128)S(1)}, f32[1,16,256]{2,1,0:T(8,128)S(1)}, u32[]{:S(2)}, u32[]{:S(2)}) collective-permute-start(f32[1,16,256]{2,1,0:T(8,128)S(1)} %broadcast.18), channel_id=1, source_target_pairs={{0,4},{4,8},{8,12},{1,5},{5,9},{9,13},{2,6},{6,10},{10,14},{3,7},{... | collective-permute-start | bytes 49160 | tf_op jit(solution)/shard_map/ppermute | solution.py:20
  55.0 11.9 %collective-permute-start.12 = (f32[1,16,256]{2,1,0:T(8,128)S(1)}, f32[1,16,256]{2,1,0:T(8,128)S(1)}, u32[]{:S(2)}, u32[]{:S(2)}) collective-permute-start(f32[1,16,256]{2,1,0:T(8,128)S(1)} %get-tuple-element.589), channel_id=1, source_target_pairs={{4,0},{8,4},{12,8},{5,1},{9,5},{13,9},{6,2},{10,6},{14,10},{7,3},{... | collective-permute-start | bytes 49160 | tf_op jit(solution)/shard_map/ppermute | solution.py:22
  56.3 10.6 %collective-permute-start.13 = (f32[1,16,256]{2,1,0:T(8,128)S(1)}, f32[1,16,256]{2,1,0:T(8,128)S(1)}, u32[]{:S(2)}, u32[]{:S(2)}) collective-permute-start(f32[1,16,256]{2,1,0:T(8,128)S(1)} %get-tuple-element.588), channel_id=1, source_target_pairs={{0,4},{4,8},{8,12},{1,5},{5,9},{9,13},{2,6},{6,10},{10,14},{3,7},{... | collective-permute-start | bytes 49160 | tf_op jit(solution)/shard_map/ppermute | solution.py:20
  61.0 11.8 %collective-permute-start.38 = (f32[34,1,256]{2,1,0:T(1,128)S(1)}, f32[34,1,256]{2,1,0:T(1,128)S(1)}, u32[]{:S(2)}, u32[]{:S(2)}) collective-permute-start(f32[34,1,256]{2,1,0:T(1,128)S(1)} %get-tuple-element.542), channel_id=1, source_target_pairs={{2,0},{3,1},{6,4},{7,5},{10,8},{11,9},{14,12},{15,13},{18,16},{19,... | collective-permute-start | bytes 104456 | tf_op jit(solution)/shard_map/ppermute | solution.py:22
  62.3 10.5 %collective-permute-start.39 = (f32[34,1,256]{2,1,0:T(1,128)S(1)}, f32[34,1,256]{2,1,0:T(1,128)S(1)}, u32[]{:S(2)}, u32[]{:S(2)}) collective-permute-start(f32[34,1,256]{2,1,0:T(1,128)S(1)} %get-tuple-element.543), channel_id=1, source_target_pairs={{0,2},{1,3},{4,6},{5,7},{8,10},{9,11},{12,14},{13,15},{16,18},{17,... | collective-permute-start | bytes 104456 | tf_op jit(solution)/shard_map/ppermute | solution.py:20
  81.3 12.9 %collective-permute-start.18 = (f32[1,16,256]{2,1,0:T(8,128)S(1)}, f32[1,16,256]{2,1,0:T(8,128)S(1)}, u32[]{:S(2)}, u32[]{:S(2)}) collective-permute-start(f32[1,16,256]{2,1,0:T(8,128)S(1)} %get-tuple-element.587), channel_id=1, source_target_pairs={{4,0},{8,4},{12,8},{5,1},{9,5},{13,9},{6,2},{10,6},{14,10},{7,3},{... | collective-permute-start | bytes 49160 | tf_op jit(solution)/shard_map/ppermute | solution.py:22
  82.6 11.6 %collective-permute-start.19 = (f32[1,16,256]{2,1,0:T(8,128)S(1)}, f32[1,16,256]{2,1,0:T(8,128)S(1)}, u32[]{:S(2)}, u32[]{:S(2)}) collective-permute-start(f32[1,16,256]{2,1,0:T(8,128)S(1)} %get-tuple-element.586), channel_id=1, source_target_pairs={{0,4},{4,8},{8,12},{1,5},{5,9},{9,13},{2,6},{6,10},{10,14},{3,7},{... | collective-permute-start | bytes 49160 | tf_op jit(solution)/shard_map/ppermute | solution.py:20
  88.2 119.6 %collective-permute-start.40 = (f32[34,18,1]{2,1,0:T(8,128)}, f32[34,18,1]{2,1,0:T(8,128)}, u32[]{:S(2)}, u32[]{:S(2)}) collective-permute-start(f32[34,18,1]{2,1,0:T(8,128)} %get-tuple-element.506), channel_id=1, source_target_pairs={{1,0},{3,2},{5,4},{7,6},{9,8},{11,10},{13,12},{15,14},{17,16},{19,... | collective-permute-start | bytes 7352 | tf_op jit(solution)/shard_map/ppermute | solution.py:22
  89.5 122.5 %collective-permute-start.41 = (f32[34,18,1]{2,1,0:T(8,128)}, f32[34,18,1]{2,1,0:T(8,128)}, u32[]{:S(2)}, u32[]{:S(2)}) collective-permute-start(f32[34,18,1]{2,1,0:T(8,128)} %get-tuple-element.507), channel_id=1, source_target_pairs={{0,1},{2,3},{4,5},{6,7},{8,9},{10,11},{12,13},{14,15},{16,17},{18,... | collective-permute-start | bytes 7352 | tf_op jit(solution)/shard_map/ppermute | solution.py:20
  94.2 7.2 %collective-permute-start.20 = (f32[34,1,256]{2,1,0:T(1,128)S(1)}, f32[34,1,256]{2,1,0:T(1,128)S(1)}, u32[]{:S(2)}, u32[]{:S(2)}) collective-permute-start(f32[34,1,256]{2,1,0:T(1,128)S(1)} %get-tuple-element.554), channel_id=1, source_target_pairs={{2,0},{3,1},{6,4},{7,5},{10,8},{11,9},{14,12},{15,13},{18,16},{19,... | collective-permute-start | bytes 104456 | tf_op jit(solution)/shard_map/ppermute | solution.py:22
  108.5 9.9 %collective-permute-start.24 = (f32[1,16,256]{2,1,0:T(8,128)S(1)}, f32[1,16,256]{2,1,0:T(8,128)S(1)}, u32[]{:S(2)}, u32[]{:S(2)}) collective-permute-start(f32[1,16,256]{2,1,0:T(8,128)S(1)} %get-tuple-element.585), channel_id=1, source_target_pairs={{4,0},{8,4},{12,8},{5,1},{9,5},{13,9},{6,2},{10,6},{14,10},{7,3},{... | collective-permute-start | bytes 49160 | tf_op jit(solution)/shard_map/ppermute | solution.py:22
  109.8 8.6 %collective-permute-start.25 = (f32[1,16,256]{2,1,0:T(8,128)S(1)}, f32[1,16,256]{2,1,0:T(8,128)S(1)}, u32[]{:S(2)}, u32[]{:S(2)}) collective-permute-start(f32[1,16,256]{2,1,0:T(8,128)S(1)} %get-tuple-element.584), channel_id=1, source_target_pairs={{0,4},{4,8},{8,12},{1,5},{5,9},{9,13},{2,6},{6,10},{10,14},{3,7},{... | collective-permute-start | bytes 49160 | tf_op jit(solution)/shard_map/ppermute | solution.py:20
  114.4 19.8 %collective-permute-start.42 = (f32[16,16,256]{2,1,0:T(8,128)S(1)}, f32[16,16,256]{2,1,0:T(8,128)S(1)}, u32[]{:S(2)}, u32[]{:S(2)}) collective-permute-start(f32[16,16,256]{2,1,0:T(8,128)S(1)} %get-tuple-element.580), channel_id=1, source_target_pairs={{0,4},{4,8},{8,12},{1,5},{5,9},{9,13},{2,6},{6,10},{10,14},{3,7},{... | collective-permute-start | bytes 786440 | tf_op jit(solution)/shard_map/ppermute | solution.py:20
  118.4 6.7 %collective-permute-start.26 = (f32[34,1,256]{2,1,0:T(1,128)S(1)}, f32[34,1,256]{2,1,0:T(1,128)S(1)}, u32[]{:S(2)}, u32[]{:S(2)}) collective-permute-start(f32[34,1,256]{2,1,0:T(1,128)S(1)} %get-tuple-element.550), channel_id=1, source_target_pairs={{2,0},{3,1},{6,4},{7,5},{10,8},{11,9},{14,12},{15,13},{18,16},{19,... | collective-permute-start | bytes 104456 | tf_op jit(solution)/shard_map/ppermute | solution.py:22
  119.7 6.7 %collective-permute-start.27 = (f32[34,1,256]{2,1,0:T(1,128)S(1)}, f32[34,1,256]{2,1,0:T(1,128)S(1)}, u32[]{:S(2)}, u32[]{:S(2)}) collective-permute-start(f32[34,1,256]{2,1,0:T(1,128)S(1)} %get-tuple-element.551), channel_id=1, source_target_pairs={{0,2},{1,3},{4,6},{5,7},{8,10},{9,11},{12,14},{13,15},{16,18},{17,... | collective-permute-start | bytes 104456 | tf_op jit(solution)/shard_map/ppermute | solution.py:20
  125.1 10.4 %collective-permute-start.43 = (f32[16,16,256]{2,1,0:T(8,128)S(1)}, f32[16,16,256]{2,1,0:T(8,128)S(1)}, u32[]{:S(2)}, u32[]{:S(2)}) collective-permute-start(f32[16,16,256]{2,1,0:T(8,128)S(1)} %get-tuple-element.581), channel_id=1, source_target_pairs={{4,0},{8,4},{12,8},{5,1},{9,5},{13,9},{6,2},{10,6},{14,10},{7,3},{... | collective-permute-start | bytes 786440 | tf_op jit(solution)/shard_map/ppermute | solution.py:22
  126.4 143.5 %collective-permute-start.56 = (f32[16,16,256]{2,1,0:T(8,128)}, f32[16,16,256]{2,1,0:T(8,128)}, u32[]{:S(2)}, u32[]{:S(2)}) collective-permute-start(f32[16,16,256]{2,1,0:T(8,128)} %get-tuple-element.574), channel_id=1, source_target_pairs={{0,4},{4,8},{8,12},{1,5},{5,9},{9,13},{2,6},{6,10},{10,14},{3,7},{... | collective-permute-start | bytes 786440 | tf_op jit(solution)/shard_map/ppermute | solution.py:20
  134.2 135.7 %collective-permute-start.57 = (f32[16,16,256]{2,1,0:T(8,128)}, f32[16,16,256]{2,1,0:T(8,128)}, u32[]{:S(2)}, u32[]{:S(2)}) collective-permute-start(f32[16,16,256]{2,1,0:T(8,128)} %get-tuple-element.575), channel_id=1, source_target_pairs={{4,0},{8,4},{12,8},{5,1},{9,5},{13,9},{6,2},{10,6},{14,10},{7,3},{... | collective-permute-start | bytes 786440 | tf_op jit(solution)/shard_map/ppermute | solution.py:22
  135.5 82.0 %collective-permute-start.28 = (f32[34,18,1]{2,1,0:T(8,128)}, f32[34,18,1]{2,1,0:T(8,128)}, u32[]{:S(2)}, u32[]{:S(2)}) collective-permute-start(f32[34,18,1]{2,1,0:T(8,128)} %get-tuple-element.510), channel_id=1, source_target_pairs={{1,0},{3,2},{5,4},{7,6},{9,8},{11,10},{13,12},{15,14},{17,16},{19,... | collective-permute-start | bytes 7352 | tf_op jit(solution)/shard_map/ppermute | solution.py:22
  207.9 14.8 %collective-permute-start.29 = (f32[34,18,1]{2,1,0:T(8,128)}, f32[34,18,1]{2,1,0:T(8,128)S(1)}, u32[]{:S(2)}, u32[]{:S(2)}) collective-permute-start(f32[34,18,1]{2,1,0:T(8,128)} %get-tuple-element.511), channel_id=1, source_target_pairs={{0,1},{2,3},{4,5},{6,7},{8,9},{10,11},{12,13},{14,15},{16,17},{18,... | collective-permute-start | bytes 7352 | tf_op jit(solution)/shard_map/ppermute | solution.py:20
  216.1 8.3 %collective-permute-start.44 = (f32[1,16,256]{2,1,0:T(8,128)S(1)}, f32[1,16,256]{2,1,0:T(8,128)S(1)}, u32[]{:S(2)}, u32[]{:S(2)}) collective-permute-start(f32[1,16,256]{2,1,0:T(8,128)S(1)} %get-tuple-element.579), channel_id=1, source_target_pairs={{4,0},{8,4},{12,8},{5,1},{9,5},{13,9},{6,2},{10,6},{14,10},{7,3},{... | collective-permute-start | bytes 49160 | tf_op jit(solution)/shard_map/ppermute | solution.py:22
  217.5 7.0 %collective-permute-start.45 = (f32[1,16,256]{2,1,0:T(8,128)S(1)}, f32[1,16,256]{2,1,0:T(8,128)S(1)}, u32[]{:S(2)}, u32[]{:S(2)}) collective-permute-start(f32[1,16,256]{2,1,0:T(8,128)S(1)} %get-tuple-element.578), channel_id=1, source_target_pairs={{0,4},{4,8},{8,12},{1,5},{5,9},{9,13},{2,6},{6,10},{10,14},{3,7},{... | collective-permute-start | bytes 49160 | tf_op jit(solution)/shard_map/ppermute | solution.py:20
  224.5 7.2 %collective-permute-start.46 = (f32[34,1,256]{2,1,0:T(1,128)S(1)}, f32[34,1,256]{2,1,0:T(1,128)S(1)}, u32[]{:S(2)}, u32[]{:S(2)}) collective-permute-start(f32[34,1,256]{2,1,0:T(1,128)S(1)} %get-tuple-element.538), channel_id=1, source_target_pairs={{2,0},{3,1},{6,4},{7,5},{10,8},{11,9},{14,12},{15,13},{18,16},{19,... | collective-permute-start | bytes 104456 | tf_op jit(solution)/shard_map/ppermute | solution.py:22
  230.4 12.9 %collective-permute-start.30 = (f32[1,16,256]{2,1,0:T(8,128)S(1)}, f32[1,16,256]{2,1,0:T(8,128)S(1)}, u32[]{:S(2)}, u32[]{:S(2)}) collective-permute-start(f32[1,16,256]{2,1,0:T(8,128)S(1)} %get-tuple-element.583), channel_id=1, source_target_pairs={{4,0},{8,4},{12,8},{5,1},{9,5},{13,9},{6,2},{10,6},{14,10},{7,3},{... | collective-permute-start | bytes 49160 | tf_op jit(solution)/shard_map/ppermute | solution.py:22
  233.6 7.5 %collective-permute-start.49 = (f32[34,18,1]{2,1,0:T(8,128)S(1)}, f32[34,18,1]{2,1,0:T(8,128)S(1)}, u32[]{:S(2)}, u32[]{:S(2)}) collective-permute-start(f32[34,18,1]{2,1,0:T(8,128)S(1)} %get-tuple-element.505), channel_id=1, source_target_pairs={{0,1},{2,3},{4,5},{6,7},{8,9},{10,11},{12,13},{14,15},{16,17},{18,... | collective-permute-start | bytes 7352 | tf_op jit(solution)/shard_map/ppermute | solution.py:20
  236.8 11.0 %collective-permute-start.31 = (f32[1,16,256]{2,1,0:T(8,128)S(1)}, f32[1,16,256]{2,1,0:T(8,128)S(1)}, u32[]{:S(2)}, u32[]{:S(2)}) collective-permute-start(f32[1,16,256]{2,1,0:T(8,128)S(1)} %get-tuple-element.582), channel_id=1, source_target_pairs={{0,4},{4,8},{8,12},{1,5},{5,9},{9,13},{2,6},{6,10},{10,14},{3,7},{... | collective-permute-start | bytes 49160 | tf_op jit(solution)/shard_map/ppermute | solution.py:20
  241.9 7.2 %collective-permute-start.50 = (f32[1,16,256]{2,1,0:T(8,128)S(1)}, f32[1,16,256]{2,1,0:T(8,128)S(1)}, u32[]{:S(2)}, u32[]{:S(2)}) collective-permute-start(f32[1,16,256]{2,1,0:T(8,128)S(1)} %get-tuple-element.577), channel_id=1, source_target_pairs={{4,0},{8,4},{12,8},{5,1},{9,5},{13,9},{6,2},{10,6},{14,10},{7,3},{... | collective-permute-start | bytes 49160 | tf_op jit(solution)/shard_map/ppermute | solution.py:22
  243.3 10.5 %collective-permute-start.51 = (f32[1,16,256]{2,1,0:T(8,128)S(1)}, f32[1,16,256]{2,1,0:T(8,128)S(1)}, u32[]{:S(2)}, u32[]{:S(2)}) collective-permute-start(f32[1,16,256]{2,1,0:T(8,128)S(1)} %get-tuple-element.576), channel_id=1, source_target_pairs={{0,4},{4,8},{8,12},{1,5},{5,9},{9,13},{2,6},{6,10},{10,14},{3,7},{... | collective-permute-start | bytes 49160 | tf_op jit(solution)/shard_map/ppermute | solution.py:20
  247.9 7.2 %collective-permute-start.32 = (f32[34,1,256]{2,1,0:T(1,128)S(1)}, f32[34,1,256]{2,1,0:T(1,128)S(1)}, u32[]{:S(2)}, u32[]{:S(2)}) collective-permute-start(f32[34,1,256]{2,1,0:T(1,128)S(1)} %get-tuple-element.546), channel_id=1, source_target_pairs={{2,0},{3,1},{6,4},{7,5},{10,8},{11,9},{14,12},{15,13},{18,16},{19,... | collective-permute-start | bytes 104456 | tf_op jit(solution)/shard_map/ppermute | solution.py:22
  249.2 10.6 %collective-permute-start.33 = (f32[34,1,256]{2,1,0:T(1,128)S(1)}, f32[34,1,256]{2,1,0:T(1,128)S(1)}, u32[]{:S(2)}, u32[]{:S(2)}) collective-permute-start(f32[34,1,256]{2,1,0:T(1,128)S(1)} %get-tuple-element.547), channel_id=1, source_target_pairs={{0,2},{1,3},{4,6},{5,7},{8,10},{9,11},{12,14},{13,15},{16,18},{17,... | collective-permute-start | bytes 104456 | tf_op jit(solution)/shard_map/ppermute | solution.py:20
  253.8 7.1 %collective-permute-start.52 = (f32[34,1,256]{2,1,0:T(1,128)S(1)}, f32[34,1,256]{2,1,0:T(1,128)S(1)}, u32[]{:S(2)}, u32[]{:S(2)}) collective-permute-start(f32[34,1,256]{2,1,0:T(1,128)S(1)} %get-tuple-element.534), channel_id=1, source_target_pairs={{2,0},{3,1},{6,4},{7,5},{10,8},{11,9},{14,12},{15,13},{18,16},{19,... | collective-permute-start | bytes 104456 | tf_op jit(solution)/shard_map/ppermute | solution.py:22
  262.7 64.8 %collective-permute-start.54 = (f32[34,18,1]{2,1,0:T(8,128)}, f32[34,18,1]{2,1,0:T(8,128)}, u32[]{:S(2)}, u32[]{:S(2)}) collective-permute-start(f32[34,18,1]{2,1,0:T(8,128)} %get-tuple-element.502), channel_id=1, source_target_pairs={{1,0},{3,2},{5,4},{7,6},{9,8},{11,10},{13,12},{15,14},{17,16},{19,... | collective-permute-start | bytes 7352 | tf_op jit(solution)/shard_map/ppermute | solution.py:22
  263.9 63.5 %collective-permute-start.55 = (f32[34,18,1]{2,1,0:T(8,128)}, f32[34,18,1]{2,1,0:T(8,128)}, u32[]{:S(2)}, u32[]{:S(2)}) collective-permute-start(f32[34,18,1]{2,1,0:T(8,128)} %get-tuple-element.503), channel_id=1, source_target_pairs={{0,1},{2,3},{4,5},{6,7},{8,9},{10,11},{12,13},{14,15},{16,17},{18,... | collective-permute-start | bytes 7352 | tf_op jit(solution)/shard_map/ppermute | solution.py:20
  333.2 10.6 %collective-permute-start.58 = (f32[1,16,256]{2,1,0:T(8,128)S(1)}, f32[1,16,256]{2,1,0:T(8,128)S(1)}, u32[]{:S(2)}, u32[]{:S(2)}) collective-permute-start(f32[1,16,256]{2,1,0:T(8,128)S(1)} %get-tuple-element.573), channel_id=1, source_target_pairs={{4,0},{8,4},{12,8},{5,1},{9,5},{13,9},{6,2},{10,6},{14,10},{7,3},{... | collective-permute-start | bytes 49160 | tf_op jit(solution)/shard_map/ppermute | solution.py:22
  334.5 9.3 %collective-permute-start.59 = (f32[1,16,256]{2,1,0:T(8,128)S(1)}, f32[1,16,256]{2,1,0:T(8,128)S(1)}, u32[]{:S(2)}, u32[]{:S(2)}) collective-permute-start(f32[1,16,256]{2,1,0:T(8,128)S(1)} %get-tuple-element.572), channel_id=1, source_target_pairs={{0,4},{4,8},{8,12},{1,5},{5,9},{9,13},{2,6},{6,10},{10,14},{3,7},{... | collective-permute-start | bytes 49160 | tf_op jit(solution)/shard_map/ppermute | solution.py:20
  339.3 24.9 %collective-permute-start.34 = (f32[34,18,1]{2,1,0:T(8,128)S(1)}, f32[34,18,1]{2,1,0:T(8,128)S(1)}, u32[]{:S(2)}, u32[]{:S(2)}) collective-permute-start(f32[34,18,1]{2,1,0:T(8,128)S(1)} %get-tuple-element.508), channel_id=1, source_target_pairs={{1,0},{3,2},{5,4},{7,6},{9,8},{11,10},{13,12},{15,14},{17,16},{19,... | collective-permute-start | bytes 7352 | tf_op jit(solution)/shard_map/ppermute | solution.py:22
  340.7 23.4 %collective-permute-start.35 = (f32[34,18,1]{2,1,0:T(8,128)S(1)}, f32[34,18,1]{2,1,0:T(8,128)S(1)}, u32[]{:S(2)}, u32[]{:S(2)}) collective-permute-start(f32[34,18,1]{2,1,0:T(8,128)S(1)} %get-tuple-element.509), channel_id=1, source_target_pairs={{0,1},{2,3},{4,5},{6,7},{8,9},{10,11},{12,13},{14,15},{16,17},{18,... | collective-permute-start | bytes 7352 | tf_op jit(solution)/shard_map/ppermute | solution.py:20
  358.3 6.8 %collective-permute-start.64 = (f32[1,16,256]{2,1,0:T(8,128)S(1)}, f32[1,16,256]{2,1,0:T(8,128)S(1)}, u32[]{:S(2)}, u32[]{:S(2)}) collective-permute-start(f32[1,16,256]{2,1,0:T(8,128)S(1)} %get-tuple-element.571), channel_id=1, source_target_pairs={{4,0},{8,4},{12,8},{5,1},{9,5},{13,9},{6,2},{10,6},{14,10},{7,3},{... | collective-permute-start | bytes 49160 | tf_op jit(solution)/shard_map/ppermute | solution.py:22
  365.6 11.4 %collective-permute-start.66 = (f32[34,1,256]{2,1,0:T(1,128)S(1)}, f32[34,1,256]{2,1,0:T(1,128)S(1)}, u32[]{:S(2)}, u32[]{:S(2)}) collective-permute-start(f32[34,1,256]{2,1,0:T(1,128)S(1)} %get-tuple-element.526), channel_id=1, source_target_pairs={{2,0},{3,1},{6,4},{7,5},{10,8},{11,9},{14,12},{15,13},{18,16},{19,... | collective-permute-start | bytes 104456 | tf_op jit(solution)/shard_map/ppermute | solution.py:22
  366.9 10.1 %collective-permute-start.67 = (f32[34,1,256]{2,1,0:T(1,128)S(1)}, f32[34,1,256]{2,1,0:T(1,128)S(1)}, u32[]{:S(2)}, u32[]{:S(2)}) collective-permute-start(f32[34,1,256]{2,1,0:T(1,128)S(1)} %get-tuple-element.527), channel_id=1, source_target_pairs={{0,2},{1,3},{4,6},{5,7},{8,10},{9,11},{12,14},{13,15},{16,18},{17,... | collective-permute-start | bytes 104456 | tf_op jit(solution)/shard_map/ppermute | solution.py:20
  371.5 13.9 %collective-permute-start.70 = (f32[16,16,256]{2,1,0:T(8,128)S(1)}, f32[16,16,256]{2,1,0:T(8,128)S(1)}, u32[]{:S(2)}, u32[]{:S(2)}) collective-permute-start(f32[16,16,256]{2,1,0:T(8,128)S(1)} %get-tuple-element.568), channel_id=1, source_target_pairs={{0,4},{4,8},{8,12},{1,5},{5,9},{9,13},{2,6},{6,10},{10,14},{3,7},{... | collective-permute-start | bytes 786440 | tf_op jit(solution)/shard_map/ppermute | solution.py:20
  375.8 9.7 %collective-permute-start.71 = (f32[16,16,256]{2,1,0:T(8,128)S(1)}, f32[16,16,256]{2,1,0:T(8,128)S(1)}, u32[]{:S(2)}, u32[]{:S(2)}) collective-permute-start(f32[16,16,256]{2,1,0:T(8,128)S(1)} %get-tuple-element.569), channel_id=1, source_target_pairs={{4,0},{8,4},{12,8},{5,1},{9,5},{13,9},{6,2},{10,6},{14,10},{7,3},{... | collective-permute-start | bytes 786440 | tf_op jit(solution)/shard_map/ppermute | solution.py:22
  378.3 78.0 %collective-permute-start.68 = (f32[34,18,1]{2,1,0:T(8,128)}, f32[34,18,1]{2,1,0:T(8,128)}, u32[]{:S(2)}, u32[]{:S(2)}) collective-permute-start(f32[34,18,1]{2,1,0:T(8,128)} %get-tuple-element.498), channel_id=1, source_target_pairs={{1,0},{3,2},{5,4},{7,6},{9,8},{11,10},{13,12},{15,14},{17,16},{19,... | collective-permute-start | bytes 7352 | tf_op jit(solution)/shard_map/ppermute | solution.py:22
  379.6 76.7 %collective-permute-start.69 = (f32[34,18,1]{2,1,0:T(8,128)}, f32[34,18,1]{2,1,0:T(8,128)}, u32[]{:S(2)}, u32[]{:S(2)}) collective-permute-start(f32[34,18,1]{2,1,0:T(8,128)} %get-tuple-element.499), channel_id=1, source_target_pairs={{0,1},{2,3},{4,5},{6,7},{8,9},{10,11},{12,13},{14,15},{16,17},{18,... | collective-permute-start | bytes 7352 | tf_op jit(solution)/shard_map/ppermute | solution.py:20
  461.5 6.6 %collective-permute-start.73 = (f32[1,16,256]{2,1,0:T(8,128)S(1)}, f32[1,16,256]{2,1,0:T(8,128)S(1)}, u32[]{:S(2)}, u32[]{:S(2)}) collective-permute-start(f32[1,16,256]{2,1,0:T(8,128)S(1)} %get-tuple-element.566), channel_id=1, source_target_pairs={{0,4},{4,8},{8,12},{1,5},{5,9},{9,13},{2,6},{6,10},{10,14},{3,7},{... | collective-permute-start | bytes 49160 | tf_op jit(solution)/shard_map/ppermute | solution.py:20
  (50 other events, 657.7 us)
where the time goes:
time: 489 us; the launch traced here: 483 us
  starting transfers between devices  217 us (44%)
  other arithmetic  135 us (28%)
  loops' own time  65.4 us (13%)
  local copies, waits for them, and re-layouts  43.2 us (9%)
  waiting for transfers between devices  19.8 us (4%)
    ppermute x39, starting transfers between devices, padded_2(): lax.ppermute(tail, axis, [(i, (i + 1) % count) for i in range(ends)])  167 us
    add x51, other arithmetic, accumulate(): return running + reflectivity[offset_index].astype(jnp.float32) * moved  97.9 us
    another operation x3, loops' own time, shards(): source = lax.fori_loop(0, NOFF, accumulate, jnp.zeros_like(current))  65.4 us
    ppermute x39, starting transfers between devices, padded_2(): lax.ppermute(head, axis, [((i + 1) % count, i) for i in range(ends)])  50.5 us
    dynamic_slice x51, local copies, waits for them, and re-layouts, accumulate(): start = MARGIN + offsets[offset_index]  31.8 us
    ppermute x39, waiting for transfers between devices, padded_2(): lax.ppermute(tail, axis, [(i, (i + 1) % count) for i in range(ends)])  16.6 us
    add x6, other arithmetic, shards(): advanced = step_single(run_wave_scat, run_scat_prior, core_coefs) + forcing  16.4 us
    concatenate x26, other arithmetic, padded_2(): jnp.concatenate([lax.ppermute(tail, axis, [(i, (i + 1) % count) for i in...  13 us
  transfers between devices with their start and end apart: 78, of which 17 were waited for; matrix products, arithmetic and copies ran while one was open for 33% of the time, Pallas kernels for 0%

commit v1 on v0

v1 whole, which is shorter than its diff:
```python
import functools

import jax
import jax.numpy as jnp
from jax import lax
from jax.experimental import pallas as pl
from jax.experimental.pallas import tpu as pltpu
from jax.sharding import PartitionSpec as P

MARGIN = 16
LANES = 128
Z0 = 8
MESH = pl.DeviceIdType.MESH
DIAGONALS = ((1, 1), (1, -1), (-1, 1), (-1, -1))
X_UP, X_DOWN, FAR_UP, FAR_DOWN, Z_UP, Z_DOWN, SIDE, DIAG = 0, 1, 2, 3, 4, 5, 6, 7
SLOTS = 11

PI_HIGH = 3.140625
PI_LOW = 9.67653589793e-4


def trig_products(tilt):
    turns = jnp.round(tilt * (1.0 / 3.14159265358979))
    t = tilt - turns * PI_HIGH
    t = t - turns * PI_LOW
    q = t * t
    s = -2.5052108e-08
    for c in (2.7557319e-06, -1.9841270e-04, 8.3333333e-03, -1.6666667e-01, 1.0):
        s = s * q + c
    s = s * t
    c_ = 2.0876757e-09
    for c in (-2.7557319e-07, 2.4801587e-05, -1.3888889e-03, 4.1666667e-02, -0.5, 1.0):
        c_ = c_ * q + c
    return s * s, c_ * c_, s * c_


def kernel(
    n_gx, n_sec, n_gy, noff,
    now_h, before_h, courant_h, aniso_h, tilt_h, refl_h, off_s,
    back_h, scat_h,
    u0, u1, u2, u3, u4, u5, u6, w1, w2, w3, w4, w5, before, coef, courant, refl, force, last,
    in_sem, out_sem, send_sem, recv_sem,
):
    X, Z = before.shape[1], before.shape[2]
    NT = before.shape[0]
    shot, gx, sec, gy = (lax.axis_index(a) for a in ("shot", "gx", "section", "gy"))
    partner = n_gy - 1 - gy
    rows = pl.ds(Z0, Z)

    def there(dx, dz):
        ok = None
        for d, i, n in ((dx, gx, n_gx), (dz, sec, n_sec)):
            if d:
                here = (i + d >= 0) & (i + d < n)
                ok = here if ok is None else ok & here
        return ok

    def device(dx, dz):
        return (shot, lax.rem(gx + dx + n_gx, n_gx), lax.rem(sec + dz + n_sec, n_sec), gy)

    side_device = (shot, gx, sec, partner)
    moves = ((1, 0), (-1, 0), (0, 1), (0, -1)) + DIAGONALS

    barrier = pltpu.get_barrier_semaphore()
    count = jnp.int32(1)
    for dx, dz in moves:
        ok = there(dx, dz)
        count += ok.astype(jnp.int32)

        @pl.when(ok)
        def _():
            pl.semaphore_signal(barrier, inc=1, device_id=device(dx, dz), device_id_type=MESH)

    pl.semaphore_signal(barrier, inc=1, device_id=side_device, device_id_type=MESH)

    def load(source, target, i):
        out = []
        for t in range(NT):
            c = pltpu.make_async_copy(
                source.at[:, :, pl.ds(t * LANES, LANES)], target(t), in_sem.at[i * NT + t]
            )
            c.start()
            out.append(c)
        return out

    ins = [
        load(now_h, lambda t: u0.at[t, pl.ds(1, X), rows, :], 0),
        load(tilt_h, lambda t: coef.at[0, t], 1),
        load(aniso_h, lambda t: coef.at[1, t], 2),
        load(courant_h, lambda t: courant.at[t], 3),
        load(before_h, lambda t: before.at[t], 4),
    ]
    refl_in = []
    for t in range(NT):
        c = pltpu.make_async_copy(
            refl_h.at[:, :, :, pl.ds(t * LANES, LANES)], refl.at[t], in_sem.at[5 * NT + t]
        )
        c.start()
        refl_in.append(c)

    def remote(src, dst, e, slot, dev):
        return pltpu.make_async_remote_copy(
            src_ref=src, dst_ref=dst,
            send_sem=send_sem.at[e * SLOTS + slot], recv_sem=recv_sem.at[e * SLOTS + slot],
            device_id=dev, device_id_type=MESH,
        )

    def pad_of(f):
        return (f.shape[1] - X) // 2

    def exchange(f, e, near=True, far=False, skip=0):
        px = pad_of(f)
        every = pl.ds(0, NT)
        xs = pl.ds(px, X)
        out = []
        if near:
            for d, slot in ((1, X_UP), (-1, X_DOWN)):
                src = px + X - 1 if d == 1 else px
                dst = px - 1 if d == 1 else px + X
                out.append((there(d, 0), there(-d, 0), remote(
                    f.at[every, pl.ds(src, 1), rows, :], f.at[every, pl.ds(dst, 1), rows, :],
                    e, slot, device(d, 0))))
            for d, slot in ((1, Z_UP), (-1, Z_DOWN)):
                src = Z0 + Z - 1 if d == 1 else Z0
                dst = Z0 - 1 if d == 1 else Z0 + Z
                out.append((there(0, d), there(0, -d), remote(
                    f.at[every, xs, pl.ds(src, 1), :], f.at[every, xs, pl.ds(dst, 1), :],
                    e, slot, device(0, d))))
            for k, (dx, dz) in enumerate(DIAGONALS):
                sx, tx = (px + X - 1, px - 1) if dx == 1 else (px, px + X)
                sz, tz = (Z0 + Z - 1, Z0 - 1) if dz == 1 else (Z0, Z0 + Z)
                out.append((there(dx, dz), there(-dx, -dz), remote(
                    f.at[every, pl.ds(sx, 1), pl.ds(sz, 1), :],
                    f.at[every, pl.ds(tx, 1), pl.ds(tz, 1), :],
                    e, DIAG + k, device(dx, dz))))
            out.append((None, None, remote(
                f.at[(NT - 1) * (1 - gy), xs, rows, :], f.at[NT, xs, rows, :],
                e, SIDE, side_device)))
        if far:
            size = MARGIN - skip
            for d, slot in ((1, FAR_UP), (-1, FAR_DOWN)):
                src = px + X - MARGIN if d == 1 else px + skip
                dst = px - MARGIN if d == 1 else px + X + skip
                out.append((there(d, 0), there(-d, 0), remote(
                    f.at[every, pl.ds(src, size), rows, :], f.at[every, pl.ds(dst, size), rows, :],
                    e, slot, device(d, 0))))
        return out

    def guarded(ok, act):
        if ok is None:
            act()
        else:
            pl.when(ok)(act)

    sent = []

    def send(copies):
        for ok, _, c in copies:
            guarded(ok, lambda c=c: c.start())
        sent.append(copies)
        return copies

    def receive(copies):
        for _, ok, c in copies:
            guarded(ok, lambda c=c: c.wait_recv())

    def clear(f, near=True):
        px = pad_of(f)
        deep = px
        for d in (1, -1):
            @pl.when(jnp.logical_not(there(d, 0)))
            def _():
                start = px + X if d == 1 else 0

                @pl.loop(0, deep)
                def _(i):
                    for t in range(NT):
                        f[t, start + i] = jnp.zeros(f.shape[2:], f.dtype)

            if near:
                @pl.when(jnp.logical_not(there(0, d)))
                def _():
                    row = Z0 + Z if d == 1 else Z0 - 1

                    @pl.loop(0, X + 2)
                    def _(i):
                        for t in range(NT):
                            f[t, px - 1 + i, pl.ds(row, 1), :] = jnp.zeros((1, LANES), f.dtype)

    lane = lax.broadcasted_iota(jnp.int32, (Z, LANES), 1)
    first, final = lane == 0, lane == LANES - 1
    has_left = jnp.full((Z, LANES), gy, jnp.int32) > 0
    turn = 1 + (LANES - 2) * (1 - gy)

    def step(f, prior, out, forcing=None):
        px = pad_of(f)

        def plane(i):
            c, s, d = [], [], []
            for t in range(NT):
                c.append(f[t, i, rows, :])
                hi = f[t, i, pl.ds(Z0 + 1, Z), :]
                lo = f[t, i, pl.ds(Z0 - 1, Z), :]
                s.append(hi + lo)
                d.append(hi - lo)
            return c, s, d

        def body(x, carry):
            cm, dm, c, s, d = carry
            cp, sp, dp = plane(px + x + 1)
            up = [pltpu.roll(v, 1, 1) for v in c]
            down = [pltpu.roll(v, LANES - 1, 1) for v in c]
            edge = pltpu.roll(f[NT, px + x, rows, :], turn, 1)
            edge_l = jnp.where(has_left, edge, 0.0)
            edge_r = jnp.where(has_left, 0.0, edge)
            for t in range(NT):
                left = jnp.where(first, up[t - 1] if t else edge_l, up[t])
                right = jnp.where(final, down[t + 1] if t < NT - 1 else edge_r, down[t])
                v = coef[0, t, x] * (cp[t] + cm[t])
                v += coef[1, t, x] * s[t]
                v += coef[2, t, x] * (left + right)
                v += coef[3, t, x] * (dp[t] - dm[t])
                v += coef[4, t, x] * c[t]
                if prior is not None:
                    v -= prior(t, x)
                if forcing is not None:
                    v += forcing(t, x)
                out(t, x, v)
            return c, d, cp, sp, dp

        cm, _, dm = plane(px - 1)
        c, s, d = plane(px)
        lax.fori_loop(0, X, body, (cm, dm, c, s, d), unroll=2)

    def reader(f):
        px = pad_of(f)
        return lambda t, x: f[t, px + x, rows, :]

    def writer(f):
        px = pad_of(f)

        def put(t, x, v):
            f[t, px + x, rows, :] = v

        return put

    def source(f, out):
        px = pad_of(f)
        starts = [off_s[h] + px for h in range(noff)]

        def body(x, carry):
            for t in range(NT):
                total = jnp.zeros((Z, LANES), jnp.float32)
                for h in range(noff):
                    total += refl[t, h, x].astype(jnp.float32) * f[t, x + starts[h], rows, :]
                out(t, x, courant[t, x] * total)
            return carry

        lax.fori_loop(0, X, body, 0)

    def plain(f):
        return lambda t, x: f[t, x]

    def put_plain(f):
        def put(t, x, v):
            f[t, x] = v

        return put

    for c in ins[0]:
        c.wait()
    pl.semaphore_wait(barrier, count)
    e0 = send(exchange(u0, 0))
    for k in (1, 2, 3, 4):
        for c in ins[k]:
            c.wait()

    def coefficients(x, carry):
        for t in range(NT):
            ss, cc, sc = trig_products(coef[0, t, x])
            e = coef[1, t, x]
            k = courant[t, x]
            stretch = 1.0 + 2.0 * e
            xx = k * (stretch * cc + ss)
            zz = k * (stretch * ss + cc)
            yy = k * stretch
            coef[0, t, x] = xx
            coef[1, t, x] = zz
            coef[2, t, x] = yy
            coef[3, t, x] = k * e * sc
            coef[4, t, x] = 2.0 - 2.0 * (xx + zz + yy)
        return carry

    lax.fori_loop(0, X, coefficients, 0, unroll=2)
    for f in (u0, u1, u2, u3, u4, u5, w1, w2, w3, w4, w5):
        clear(f)
    clear(u6, near=False)

    receive(e0)
    step(u0, plain(before), writer(u1))
    e1 = send(exchange(u1, 1))
    receive(e1)
    step(u1, reader(u0), writer(u2))
    e2 = send(exchange(u2, 2))
    far2 = send(exchange(u2, 2, near=False, far=True, skip=1))
    receive(e2)
    step(u2, reader(u1), writer(u3))
    e3 = send(exchange(u3, 3))
    for c in refl_in:
        c.wait()
    receive(e3)
    step(u3, reader(u2), writer(u4))
    e4 = send(exchange(u4, 4))
    far4 = send(exchange(u4, 4, near=False, far=True, skip=1))
    receive(far2)
    source(u2, writer(w1))
    g1 = send(exchange(w1, 7))
    receive(e4)
    step(u4, reader(u3), writer(u5))
    e5 = send(exchange(u5, 5))
    receive(g1)
    step(w1, None, writer(w2), reader(w1))
    g2 = send(exchange(w2, 8))
    receive(e5)
    step(u5, reader(u4), writer(u6))
    far6 = send(exchange(u6, 6, near=False, far=True))
    outs = []
    for t in range(NT):
        c = pltpu.make_async_copy(
            u6.at[t, pl.ds(MARGIN, X), rows, :], back_h.at[:, :, pl.ds(t * LANES, LANES)], out_sem.at[t]
        )
        c.start()
        outs.append(c)
    receive(far4)
    source(u4, put_plain(force))
    receive(g2)
    step(w2, reader(w1), writer(w3), plain(force))
    g3 = send(exchange(w3, 9))
    receive(g3)
    step(w3, reader(w2), writer(w4), plain(force))
    g4 = send(exchange(w4, 10))
    receive(far6)
    source(u6, put_plain(force))
    receive(g4)
    step(w4, reader(w3), writer(w5), plain(force))
    g5 = send(exchange(w5, 11))
    receive(g5)
    step(w5, reader(w4), put_plain(last), plain(force))
    for t in range(NT):
        c = pltpu.make_async_copy(
            last.at[t], scat_h.at[:, :, pl.ds(t * LANES, LANES)], out_sem.at[NT + t]
        )
        c.start()
        outs.append(c)
    for copies in sent:
        for ok, _, c in copies:
            guarded(ok, lambda c=c: c.wait_send())
    for c in outs:
        c.wait()


def shards(sizes, wave_now, wave_before, courant, anisotropy, tilt, reflectivity, offsets):
    X, Z, Y = wave_now.shape
    noff = reflectivity.shape[0]
    NT = Y // LANES
    f32 = jnp.float32
    thin = pltpu.VMEM((NT + 1, X + 2, Z + 2 * Z0, LANES), f32)
    wide = pltpu.VMEM((NT + 1, X + 2 * MARGIN, Z + 2 * Z0, LANES), f32)
    block = pltpu.VMEM((NT, X, Z, LANES), f32)
    exchanges = 12
    any_ = pl.BlockSpec(memory_space=pl.ANY)
    shape = jax.ShapeDtypeStruct(wave_now.shape, f32)
    return pl.pallas_call(
        functools.partial(kernel, *sizes, noff),
        out_shape=(shape, shape),
        in_specs=[any_] * 6 + [pl.BlockSpec(memory_space=pltpu.SMEM)],
        out_specs=(any_, any_),
        scratch_shapes=[
            thin, thin, wide, thin, wide, thin, wide,
            thin, thin, thin, thin, thin,
            block,
            pltpu.VMEM((5, NT, X, Z, LANES), f32),
            block,
            pltpu.VMEM((NT, noff, X, Z, LANES), jnp.bfloat16),
            block, block,
            pltpu.SemaphoreType.DMA((6 * NT,)),
            pltpu.SemaphoreType.DMA((2 * NT,)),
            pltpu.SemaphoreType.DMA((exchanges * SLOTS,)),
            pltpu.SemaphoreType.DMA((exchanges * SLOTS,)),
        ],
        compiler_params=pltpu.CompilerParams(
            collective_id=0, has_side_effects=True, vmem_limit_bytes=56 * 1024 * 1024
        ),
    )(wave_now, wave_before, courant, anisotropy, tilt, reflectivity, offsets)


def solution(mesh):
    field = P(("shot", "gx"), "section", "gy")
    sizes = tuple(mesh.shape[a] for a in ("gx", "section", "gy"))
    return jax.shard_map(
        functools.partial(shards, sizes),
        mesh=mesh,
        in_specs=(field, field, field, field, field, P(None, ("shot", "gx"), "section", "gy"), P()),
        out_specs=(field, field),
        check_vma=False,
    )
```

time: 489 us -> 61.1 us (0.12); the launches traced: 483 us -> 60.9 us
  starting transfers between devices: 217 us -> 0 us
  other arithmetic: 135 us -> 0 us
  loops' own time: 65.4 us -> 0 us
  Pallas kernels: 0 us -> 56.5 us
  local copies, waits for them, and re-layouts: 43.2 us -> 3.74 us
  waiting for transfers between devices: 19.8 us -> 0 us
    ppermute x78 -> x0, starting transfers between devices: 217 us -> none  [the longest x39 167 us: padded_2(): lax.ppermute(tail, axis, [(i, (i + 1) % count) for i in range(ends)])]
    add x63 -> x0, other arithmetic: 122 us -> none  [the longest x51 97.9 us: accumulate(): return running + reflectivity[offset_index].astype(jnp.float32) * moved]
    another operation x3 -> x0, loops' own time: 65.4 us -> none  [shards(): source = lax.fori_loop(0, NOFF, accumulate, jnp.zeros_like(current))]
    pallas_call x0 -> x1, Pallas kernels: none -> 56.5 us  [shards(): pl.pallas_call(functools.partial(kernel, *sizes, noff), out_shape=(shape,...]
    dynamic_slice x51 -> x0, local copies, waits for them, and re-layouts: 31.8 us -> none  [accumulate(): start = MARGIN + offsets[offset_index]]
    ppermute x78 -> x0, waiting for transfers between devices: 19.8 us -> none  [the longest x39 16.6 us: padded_2(): lax.ppermute(tail, axis, [(i, (i + 1) % count) for i in range(ends)])]
    concatenate x26 -> x0, other arithmetic: 13 us -> none  [padded_2(): jnp.concatenate([lax.ppermute(tail, axis, [(i, (i + 1) % count) for i in...]
    slice x27 -> x0, local copies, waits for them, and re-layouts: 7.59 us -> none  [the longest x14 6.65 us: padded_2(): head = lax.slice_in_dim(cells, 0, width, axis=dim)]
  transfers between devices with their start and end apart: 78 -> 0, of which waited for: 17 -> 0; matrix products, arithmetic and copies ran while one was open for 33% -> 0% of each run, Pallas kernels for 0% -> 0%
where the time goes in v1:
time: 61.1 us; the launch traced here: 60.9 us
  Pallas kernels  56.5 us (92%)
  local copies, waits for them, and re-layouts  3.74 us (6%)
  between operations  0.64 us (1%)
    pallas_call x1, Pallas kernels, shards(): pl.pallas_call(functools.partial(kernel, *sizes, noff), out_shape=(shape,...  56.5 us
    unnamed x2, local copies, waits for them, and re-layouts  3.74 us

profile of v1, /device:TPU:0, one launch (start us, length us, event | category | flops | bytes accessed | tf_op | source)
XLA Modules:
  0.0 60.9 jit_solution(16361366651985137295)
XLA Ops:
  0.6 56.5 %shard_map.86 = (f32[32,16,256]{2,1,0:T(8,128)}, f32[32,16,256]{2,1,0:T(8,128)}) custom-call(f32[32,16,256]{2,1,0:T(8,128)} %now_h.1, f32[32,16,256]{2,1,0:T(8,128)} %before_h.1, f32[32,16,256]{2,1,0:T(8,128)} %courant_h.1, f32[32,16,256]{2,1,0:T(8,128)} %aniso_h.1, f32[32,16,256]{2,1,0:T(8,128)} %tilt_h.1, bf16[17,32,16,256]{3,2,1,0:T(8,128)(2,1)} %refl_h.1, ...), custom_call_target="tpu_custom_call" | custom-call | tf_op jit(solution)/shard_map/pallas_call | solution.py:373
  57.1 1.9 %copy.11 = f32[32,16,256]{2,1,0:T(8,128)} copy(f32[32,16,256]{2,1,0:T(8,128)} %get-tuple-element.4) | data formatting | bytes 1048576
  59.0 1.9 %copy.12 = f32[32,16,256]{2,1,0:T(8,128)} copy(f32[32,16,256]{2,1,0:T(8,128)} %get-tuple-element.5) | data formatting | bytes 1048576

commit v2 on v1

--- a/solution.py
+++ b/solution.py
@@ -230,7 +230,7 @@
 
         cm, _, dm = plane(px - 1)
         c, s, d = plane(px)
-        lax.fori_loop(0, X, body, (cm, dm, c, s, d), unroll=2)
+        lax.fori_loop(0, X, body, (cm, dm, c, s, d), unroll=16)
 
     def reader(f):
         px = pad_of(f)
@@ -256,7 +256,7 @@
                 out(t, x, courant[t, x] * total)
             return carry
 
-        lax.fori_loop(0, X, body, 0)
+        lax.fori_loop(0, X, body, 0, unroll=2)
 
     def plain(f):
         return lambda t, x: f[t, x]
@@ -359,6 +359,19 @@
         c.wait()
 
 
+def hand_over(pieces, a, b, a_out, b_out, sem):
+    size = a.shape[0] // pieces
+    copies = []
+    for k, (src, dst) in enumerate(((a, a_out), (b, b_out))):
+        for i in range(pieces):
+            part = pl.ds(i * size, size)
+            copies.append(pltpu.make_async_copy(src.at[part], dst.at[part], sem.at[k * pieces + i]))
+    for c in copies:
+        c.start()
+    for c in copies:
+        c.wait()
+
+
 def shards(sizes, wave_now, wave_before, courant, anisotropy, tilt, reflectivity, offsets):
     X, Z, Y = wave_now.shape
     noff = reflectivity.shape[0]
@@ -370,7 +383,7 @@
     exchanges = 12
     any_ = pl.BlockSpec(memory_space=pl.ANY)
     shape = jax.ShapeDtypeStruct(wave_now.shape, f32)
-    return pl.pallas_call(
+    fields = pl.pallas_call(
         functools.partial(kernel, *sizes, noff),
         out_shape=(shape, shape),
         in_specs=[any_] * 6 + [pl.BlockSpec(memory_space=pltpu.SMEM)],
@@ -392,6 +405,15 @@
             collective_id=0, has_side_effects=True, vmem_limit_bytes=56 * 1024 * 1024
         ),
     )(wave_now, wave_before, courant, anisotropy, tilt, reflectivity, offsets)
+    pieces = 4
+    return pl.pallas_call(
+        functools.partial(hand_over, pieces),
+        out_shape=(shape, shape),
+        in_specs=[any_] * 2,
+        out_specs=(any_, any_),
+        scratch_shapes=[pltpu.SemaphoreType.DMA((2 * pieces,))],
+        cost_estimate=pl.CostEstimate(flops=0, bytes_accessed=16 * X * Z * Y, transcendentals=0),
+    )(*fields)
 
 
 def solution(mesh):

time: 61.1 us -> 81.3 us (1.33)
  Pallas kernels: 56.5 us -> 80.5 us
  local copies, waits for them, and re-layouts: 3.74 us -> 0 us
    pallas_call x0 -> x1, Pallas kernels: none -> 32.9 us  [shards(): pl.pallas_call(functools.partial(hand_over, pieces), out_shape=(shape, sh...]
    pallas_call x1, Pallas kernels: 56.5 us -> 47.6 us  [shards(): pl.pallas_call(functools.partial(kernel, *sizes, noff), out_shape=(shape,...]
    unnamed x2 -> x0, local copies, waits for them, and re-layouts: 3.74 us -> none
where the time goes in v2:
time: 81.3 us; the launch traced here: 81.1 us
  Pallas kernels  80.5 us (99%)
    pallas_call x1, Pallas kernels, shards(): pl.pallas_call(functools.partial(kernel, *sizes, noff), out_shape=(shape,...  47.6 us
    pallas_call x1, Pallas kernels, shards(): pl.pallas_call(functools.partial(hand_over, pieces), out_shape=(shape, sh...  32.9 us

profile of v2, /device:TPU:0, one launch (start us, length us, event | category | flops | bytes accessed | tf_op | source)
XLA Modules:
  0.0 81.1 jit_solution(4039417930980700580)
XLA Ops:
  0.6 47.6 %shard_map.86 = (f32[32,16,256]{2,1,0:T(8,128)}, f32[32,16,256]{2,1,0:T(8,128)}) custom-call(f32[32,16,256]{2,1,0:T(8,128)} %now_h.1, f32[32,16,256]{2,1,0:T(8,128)} %before_h.1, f32[32,16,256]{2,1,0:T(8,128)} %courant_h.1, f32[32,16,256]{2,1,0:T(8,128)} %aniso_h.1, f32[32,16,256]{2,1,0:T(8,128)} %tilt_h.1, bf16[17,32,16,256]{3,2,1,0:T(8,128)(2,1)} %refl_h.1, ...), custom_call_target="tpu_custom_call" | custom-call | tf_op jit(solution)/shard_map/pallas_call | solution.py:386
  48.2 32.9 %shard_map.87 = (f32[32,16,256]{2,1,0:T(8,128)}, f32[32,16,256]{2,1,0:T(8,128)}) custom-call(f32[32,16,256]{2,1,0:T(8,128)} %get-tuple-element.4.a, f32[32,16,256]{2,1,0:T(8,128)} %get-tuple-element.5.b), custom_call_target="tpu_custom_call" | custom-call | bytes 2097152 | tf_op jit(solution)/shard_map/pallas_call | solution.py:409
